TPU v7x, 32 devices: a whole 2x2x4 slice. The times are simulated.
32 devices in a mesh: ctx: 2 (over y), exp: 16 (over z, x, core).
Axes of the slice: x: 2, y: 2, z: 4, core: 2. Of those that a mesh axis runs over, the one named last changes fastest.
Arguments:
- inputs: bfloat16 [1536, 1024], P('exp', 'ctx'), may hold values from -6 to 6
- pre_act: bfloat16 [1536, 1024], P('exp', 'ctx'), may hold values from -6 to 6
- grad_out: bfloat16 [1536, 1024], P('exp', 'ctx'), may hold values from -6 to 6
- conv_weight: bfloat16 [5, 1536, 1536], P(None, 'exp', 'ctx'), may hold values from -0.0625 to 0.0625
- expert_ids: int32 [1024, 2], P('ctx'), may hold values from 0 to 15, as said below
- gate_values: float32 [1024, 2], P('ctx'), may hold values from 0.1 to 0.9
- expert_in: bfloat16 [16, 1536, 3072], P('exp', None, 'ctx'), may hold values from -0.15625 to 0.15625
- expert_out: bfloat16 [16, 3072, 1536], P('exp', 'ctx'), may hold values from -0.109375 to 0.109375
Outputs:
- grad_inputs: bfloat16 [1536, 1024], P('exp', 'ctx')
- grad_conv: float32 [5, 1536, 1536], P(None, 'exp', 'ctx')
- grad_expert_in: bfloat16 [16, 1536, 3072], P('exp', None, 'ctx')
- grad_expert_out: bfloat16 [16, 3072, 1536], P('exp', 'ctx')
Inputs may be any that keep to these rules, and one draw needn't show every extreme that they name: `expert_ids`: the 2 ids of a bin differ. In each aligned block of 512 bins (the bins of one index of ctx) no expert is named more than 128 times, and one expert, the same in every block, is named exactly 128 times in each block.
All inputs are finite; a program needn't handle non-finite values.
Results may differ from a plain program's by a relative error of at most 0.009.
Values may be sent and summed in bfloat16 or wider, within the bound.
A program may use at most 128 MiB of HBM per device.

v0:
```python
import jax
import jax.numpy as jnp
from jax import lax
from jax.sharding import PartitionSpec as P


def with_halo(cells, sides, width):
    for axis, dim in sides:
        count = lax.axis_size(axis)
        ends = count - 1
        head = lax.slice_in_dim(cells, 0, width, axis=dim)
        tail = lax.slice_in_dim(cells, cells.shape[dim] - width, cells.shape[dim], axis=dim)
        cells = jnp.concatenate(
            [
                lax.ppermute(tail, axis, [(i, (i + 1) % count) for i in range(ends)]),
                cells,
                lax.ppermute(head, axis, [((i + 1) % count, i) for i in range(ends)]),
            ],
            axis=dim,
        )
    return cells


def gelu_value(values):
    factor = 0.7978845608028654
    return 0.5 * values * (1.0 + jnp.tanh(factor * (values + 0.044715 * values * values * values)))


def gelu_slope(values):
    factor = 0.7978845608028654
    tangent = jnp.tanh(factor * (values + 0.044715 * values * values * values))
    return 0.5 * (1.0 + tangent) + 0.5 * values * (1.0 - tangent * tangent) * factor * (
        1.0 + 0.134145 * values * values
    )


def turned(left, right, dims):
    return lax.dot_general(
        left.astype(jnp.float32),
        right.astype(jnp.float32),
        (dims, ((), ())),
        preferred_element_type=jnp.float32,
    )


def expert_pass(w_first, w_second, rows_in, rows_grad):
    hidden = turned(w_first, rows_in, ((0,), (0,)))
    squashed = gelu_value(hidden).astype(jnp.bfloat16)
    grad_second = turned(squashed, rows_grad, ((1,), (1,)))
    grad_hidden = jnp.dot(w_second, rows_grad, preferred_element_type=jnp.float32)
    grad_pre = (grad_hidden * gelu_slope(hidden)).astype(jnp.bfloat16)
    grad_first = turned(rows_in, grad_pre, ((1,), (1,)))
    grad_rows = jnp.dot(w_first, grad_pre, preferred_element_type=jnp.float32)
    return (grad_first, grad_second, grad_rows)


def local(inputs, pre_act, grad_out, conv_weight, expert_ids, gate_values, expert_in, expert_out):
    channels, bins_local = inputs.shape
    experts = lax.axis_size("exp")
    groups = lax.axis_size("ctx")
    capacity = 4 * bins_local // experts
    model_width = channels * experts
    kernel = conv_weight.shape[0]
    margin = kernel // 2
    pre_float = pre_act.astype(jnp.float32)
    activated = (inputs.astype(jnp.float32) + gelu_value(pre_float)).astype(jnp.bfloat16)
    grad_float = grad_out.astype(jnp.float32)
    flat_ids = expert_ids.reshape(-1)
    onehot = (flat_ids[:, None] == jnp.arange(experts, dtype=jnp.int32)[None, :]).astype(jnp.int32)
    slot_index = jnp.sum(onehot * jnp.cumsum(onehot, axis=0), axis=1) - 1
    targets = flat_ids * capacity + slot_index
    owners = jnp.arange(flat_ids.shape[0], dtype=jnp.int32) // expert_ids.shape[1]
    row_table = jnp.full((experts * capacity,), bins_local, jnp.int32).at[targets].set(owners)
    gate_table = (
        jnp.zeros((experts * capacity,), jnp.float32).at[targets].set(gate_values.reshape(-1))
    )
    act_pad = jnp.concatenate([activated, jnp.zeros((channels, 1), jnp.bfloat16)], axis=1)
    grad_pad = jnp.concatenate([grad_float, jnp.zeros((channels, 1), jnp.float32)], axis=1)
    send_rows = act_pad[:, row_table].reshape(channels, experts, capacity)
    send_grad = (
        (grad_pad[:, row_table] * gate_table[None, :])
        .astype(jnp.bfloat16)
        .reshape(channels, experts, capacity)
    )
    weight_first = expert_in[0]
    weight_second = expert_out[0]
    total_rows = groups * capacity
    copied = (
        lax.all_gather(send_rows, "ctx", axis=2, tiled=True),
        lax.all_gather(send_grad, "ctx", axis=2, tiled=True),
    )
    arrived = (
        lax.all_to_all(copied[0], "exp", split_axis=1, concat_axis=0, tiled=True),
        lax.all_to_all(copied[1], "exp", split_axis=1, concat_axis=0, tiled=True),
    )
    part_in, part_out, part_rows = expert_pass(
        weight_first, weight_second, arrived[0][:, 0, :], arrived[1][:, 0, :]
    )
    rows_back = part_rows
    sum_first, sum_second, rows_back = (part_in, part_out, rows_back)
    moved_back = lax.all_to_all(
        rows_back.reshape(model_width, 1, total_rows),
        "exp",
        split_axis=0,
        concat_axis=1,
        tiled=True,
    )
    returned = lax.psum_scatter(moved_back, "ctx", scatter_dimension=2, tiled=True).astype(
        jnp.bfloat16
    )
    back_flat = returned.reshape(channels, experts * capacity).astype(jnp.float32)
    per_bin = targets.reshape(bins_local, -1)
    grad_total = grad_float
    for column in range(per_bin.shape[1]):
        grad_total = grad_total + back_flat[:, per_bin[:, column]]
    grad_pre_conv = (grad_total * gelu_slope(pre_float)).astype(jnp.bfloat16)
    full_weight = lax.all_gather(conv_weight, "ctx", axis=2, tiled=True)
    rim_inputs = with_halo(inputs, (("ctx", 1),), margin)
    gathered = lax.all_gather(grad_pre_conv, "exp", axis=0, tiled=True)
    rim_grad = with_halo(gathered, (("ctx", 1),), margin)
    conv_back = jnp.zeros((channels, bins_local), jnp.float32)
    tap_grads = []
    for offset in range(kernel):
        lower = 2 * margin - offset
        weight_cols = full_weight[offset]
        conv_back = conv_back + jnp.dot(
            weight_cols, rim_grad[:, lower : lower + bins_local], preferred_element_type=jnp.float32
        )
        tap_grads.append(
            turned(
                rim_inputs[:, offset : offset + bins_local],
                rim_grad[:, margin : margin + bins_local],
                ((1,), (1,)),
            )
        )
    conv_grad = jnp.stack(tap_grads)
    conv_back, conv_grad = (conv_back, conv_grad)
    grad_inputs = (grad_total + conv_back).astype(jnp.bfloat16)
    grad_conv = lax.psum_scatter(
        conv_grad.astype(jnp.bfloat16), "ctx", scatter_dimension=2, tiled=True
    ).astype(jnp.float32)
    return (
        grad_inputs,
        grad_conv,
        sum_first.astype(jnp.bfloat16)[None],
        sum_second.astype(jnp.bfloat16)[None],
    )


def solution(mesh):
    placed = (
        P("exp", "ctx"),
        P("exp", "ctx"),
        P("exp", "ctx"),
        P(None, "exp", "ctx"),
        P("ctx", None),
        P("ctx", None),
        P("exp", None, "ctx"),
        P("exp", "ctx", None),
    )
    return jax.shard_map(
        local,
        mesh=mesh,
        in_specs=placed,
        out_specs=(
            P("exp", "ctx"),
            P(None, "exp", "ctx"),
            P("exp", None, "ctx"),
            P("exp", "ctx", None),
        ),
        check_vma=False,
    )
```

profile of v0, /device:TPU:0, one launch (start us, length us, event | category | flops | bytes accessed | tf_op | source)
XLA Modules:
  0.0 288.9 jit_solution(6828851017552488800)
XLA Ops:
  8.4 4.5 %reduce-window.6 = s32[16,8,128]{2,1,0:T(8,128)S(1)} reduce-window(s32[16,8,128]{2,1,0:T(8,128)S(1)} %fusion.94, s32[]{:T(128)} %constant.17.clone.1), window={size=1x1x128 pad=0_0x0_0x127_0}, to_apply=%region_0.0 | reduce-window | flops 2080768 | bytes 131076 | tf_op jit(solution)/shard_map/reduce-window
  13.8 4.3 %scatter_custom_fusion = s32[2048]{0:T(1024)S(1)} fusion(s32[1024]{0:T(1024)S(1)} %bitcast.156, s32[1024]{0:T(1024)S(1)} %add_select_fusion, s32[]{:T(128)} %constant.15.clone.1), kind=kCustom, calls=%fused_computation.131 | custom fusion | bytes 8196 | tf_op jit(solution)/shard_map/scatter | solution.py:73
  18.5 6.2 %gather_fusion.1 = bf16[2048,96]{1,0:T(8,128)(2,1)S(1)} fusion(bf16[96,513]{0,1:T(8,128)(2,1)S(1)} %concatenate.25.clone, s32[2048]{0:T(1024)S(1)} %fusion.95), kind=kCustom, calls=%fused_computation.1 | custom fusion | bytes 794624 | tf_op jit(solution)/shard_map/gather | solution.py:79
  24.9 13.0 %all_gather.13 = bf16[96,16,256]{2,0,1:T(8,128)(2,1)} all-gather(bf16[96,16,128]{2,0,1:T(8,128)(2,1)S(1)} %copy.56), channel_id=1, replica_groups=mesh['ctx'=2,'exp'=16] {'ctx'}, dimensions={2}, use_global_device_ids=true | all-gather | bytes 1179648 | tf_op jit(solution)/shard_map/all_gather | solution.py:89
  37.9 6.2 %all-to-all-start.1 = ((bf16[96,16,256]{2,0,1:T(8,128)(2,1)}), bf16[96,16,256]{2,0,1:T(8,128)(2,1)S(1)}, u32[]{:S(2)}, u32[]{:S(2)}) async-start(bf16[96,16,256]{2,0,1:T(8,128)(2,1)} %all_gather.13), calls=%async_computation.1 | async-start | bytes 1572864 | tf_op jit(solution)/shard_map/all_to_all | solution.py:93
  44.2 5.5 %gather_fusion = f32[2048,96]{1,0:T(8,128)S(1)} fusion(f32[96,513]{0,1:T(8,128)S(1)} %concatenate.24.clone, s32[2048]{0:T(1024)S(1)} %fusion.95), kind=kCustom, calls=%fused_computation | custom fusion | bytes 1581056 | tf_op jit(solution)/shard_map/gather | solution.py:81
  50.7 4.3 %scatter_custom_fusion.1 = f32[2048]{0:T(1024)S(1)} fusion(s32[1024]{0:T(1024)S(1)} %bitcast.157, f32[1024]{0:T(1024)S(1)} %reshape.134, f32[]{:T(128)} %constant.14.clone.1), kind=kCustom, calls=%fused_computation.129 | custom fusion | bytes 8196 | tf_op jit(solution)/shard_map/scatter | solution.py:75
  55.1 12.2 %all_gather.12 = bf16[96,16,256]{2,0,1:T(8,128)(2,1)} all-gather(bf16[96,16,128]{2,0,1:T(8,128)(2,1)S(1)} %multiply_convert_fusion.2), channel_id=1, replica_groups=mesh['ctx'=2,'exp'=16] {'ctx'}, dimensions={2}, use_global_device_ids=true | all-gather | bytes 1179648 | tf_op jit(solution)/shard_map/all_gather | solution.py:90
  67.3 5.7 %all-to-all-start = ((bf16[96,16,256]{2,0,1:T(8,128)(2,1)}), bf16[96,16,256]{2,0,1:T(8,128)(2,1)S(1)}, u32[]{:S(2)}, u32[]{:S(2)}) async-start(bf16[96,16,256]{2,0,1:T(8,128)(2,1)} %all_gather.12), calls=%async_computation | async-start | bytes 1572864 | tf_op jit(solution)/shard_map/all_to_all | solution.py:94
  73.1 4.9 %fusion.14 = f32[1536,256]{0,1:T(8,128)} fusion(bf16[1536,256]{1,0:T(8,128)(2,1)S(1)} %bitcast.148, bf16[1,1536,1536]{2,1,0:T(8,128)(2,1)} %param.14), kind=kOutput, calls=%fused_computation.18 | convolution fusion | flops 1207959552 | bytes 7077888 | tf_op jit(solution)/shard_map/dot_general | solution.py:38
  78.0 13.8 %all-to-all-done = bf16[96,16,256]{2,0,1:T(8,128)(2,1)S(1)} async-done(((bf16[96,16,256]{2,0,1:T(8,128)(2,1)}), bf16[96,16,256]{2,0,1:T(8,128)(2,1)S(1)}, u32[]{:S(2)}, u32[]{:S(2)}) %all-to-all-start) | async-done | bytes 786464 | tf_op jit(solution)/shard_map/all_to_all | solution.py:94
  91.8 5.1 %fusion.20 = bf16[1536,256]{0,1:T(8,128)(2,1)S(1)} fusion(bf16[1536,256]{1,0:T(8,128)(2,1)S(1)} %bitcast.150, bf16[1,1536,1536]{2,1,0:T(8,128)(2,1)} %param.15, f32[1536,256]{0,1:T(8,128)} %fusion.14), kind=kOutput, calls=%fused_computation.20 | convolution fusion | flops 1215430656 | bytes 7864320 | tf_op jit(solution)/shard_map/dot_general | solution.py:50
  97.8 4.9 %fusion.17 = f32[1536,1,256]{0,2,1:T(8,128)} fusion(bf16[1536,256]{0,1:T(8,128)(2,1)S(1)} %fusion.20, bf16[1,1536,1536]{2,1,0:T(8,128)(2,1)} %param.14), kind=kOutput, calls=%fused_computation.19 | convolution fusion | flops 1207959552 | bytes 7077888 | tf_op jit(solution)/shard_map/dot_general | solution.py:53
  102.7 3.6 %copy.57 = f32[1536,1,256]{2,1,0:T(1,128)S(1)} copy(f32[1536,1,256]{0,2,1:T(8,128)} %fusion.17) | data formatting | bytes 3145728 | tf_op jit(solution)/shard_map/reshape | solution.py:102
  106.3 41.4 %all_to_all.48 = f32[1536,1,256]{2,1,0:T(1,128)S(1)} all-to-all(f32[1536,1,256]{2,1,0:T(1,128)S(1)} %copy.57), channel_id=1, replica_groups=mesh['ctx'=2,'exp'=16] {'exp'}, dimensions={0} | all-to-all | bytes 3145728 | tf_op jit(solution)/shard_map/all_to_all | solution.py:101
  149.3 26.2 %reduce-scatter.3.cloned.1.call-done = f32[96,16,128]{2,0,1:T(8,128)} async-done(((f32[96,16,256]{2,0,1:T(8,128)}), f32[96,16,128]{2,0,1:T(8,128)}) %reduce-scatter.3.cloned.1.call-update) | async-done | bytes 786448 | tf_op jit(solution)/shard_map/reduce_scatter | solution.py:108
  184.2 4.1 %collective-permute-done.3 = bf16[96,2]{1,0:T(8,128)(2,1)S(1)} collective-permute-done((bf16[96,2]{1,0:T(8,128)(2,1)S(1)}, bf16[96,2]{1,0:T(8,128)(2,1)S(1)}, u32[]{:S(2)}, u32[]{:S(2)}) %collective-permute-start.3) | collective-permute-done | bytes 416 | tf_op jit(solution)/shard_map/ppermute | solution.py:17
  188.3 31.7 %all-gather.3.cloned.1.call-done = bf16[1536,512]{1,0:T(8,128)(2,1)} async-done(((bf16[96,512]{1,0:T(8,128)(2,1)}), bf16[1536,512]{1,0:T(8,128)(2,1)}) %all-gather.3.cloned.1.call-update) | async-done | bytes 1572880 | tf_op jit(solution)/shard_map/all_gather | solution.py:119
  220.1 2.9 fusion.24
  228.3 4.9 %fusion = bf16[1,1536,1536]{2,1,0:T(8,128)(2,1)} fusion(bf16[1536,256]{1,0:T(8,128)(2,1)S(1)} %bitcast.149, bf16[1536,256]{0,1:T(8,128)(2,1)} %copy-done.13), kind=kOutput, calls=%fused_computation.8 | convolution fusion | flops 1210318848 | bytes 6291456 | tf_op jit(solution)/shard_map/dot_general | solution.py:38
  233.2 3.9 %fusion.1 = bf16[1,1536,1536]{2,1,0:T(8,128)(2,1)} fusion(bf16[1536,256]{1,0:T(8,128)(2,1)S(1)} %bitcast.151, f32[1536,256]{0,1:T(8,128)S(1)} %copy-done.14), kind=kOutput, calls=%fused_computation.9 | convolution fusion | flops 1213857792 | bytes 7077888 | tf_op jit(solution)/shard_map/dot_general | solution.py:38
  239.5 6.0 %collective-permute-start.1 = (bf16[1536,2]{1,0:T(8,128)(2,1)}, bf16[1536,2]{1,0:T(8,128)(2,1)}, u32[]{:S(2)}, u32[]{:S(2)}) collective-permute-start(bf16[1536,2]{1,0:T(8,128)(2,1)} %get-tuple-element.7), channel_id=1, source_target_pairs={{0,16},{1,17},{2,18},{3,19},{4,20},{5,21},{6,22},{7,23},{8,24},{9,... | collective-permute-start | bytes 18440 | tf_op jit(solution)/shard_map/ppermute | solution.py:15
  245.6 4.5 %all-gather.5.cloned.1.call-done = bf16[5,96,1536]{2,1,0:T(8,128)(2,1)} async-done(((bf16[5,96,768]{2,1,0:T(8,128)(2,1)}), bf16[5,96,1536]{2,1,0:T(8,128)(2,1)}) %all-gather.5.cloned.1.call-update) | async-done | bytes 1474576 | tf_op jit(solution)/shard_map/all_gather | solution.py:117
  260.5 19.5 %reduce-scatter.5.cloned.1.call-done = bf16[5,96,768]{2,1,0:T(8,128)(2,1)} async-done(((bf16[5,96,1536]{2,1,0:T(8,128)(2,1)}), bf16[5,96,768]{2,1,0:T(8,128)(2,1)}) %reduce-scatter.5.cloned.1.call-update) | async-done | bytes 737296 | tf_op jit(solution)/shard_map/reduce_scatter | solution.py:139
  (99 shorter events, 35.4 us)
Async XLA Ops:
  7.2 11.0 %copy-start.1 = (bf16[96,512]{1,0:T(8,128)(2,1)S(1)}, bf16[96,512]{1,0:T(8,128)(2,1)}, u32[]{:S(2)}) copy-start(bf16[96,512]{1,0:T(8,128)(2,1)} %param.8) | copy-start | bytes 294916
  7.2 11.0 %copy-start.8 = (bf16[96,512]{1,0:T(8,128)(2,1)S(1)}, bf16[96,512]{1,0:T(8,128)(2,1)}, u32[]{:S(2)}) copy-start(bf16[96,512]{1,0:T(8,128)(2,1)} %param.9) | copy-start | bytes 294916
  24.9 19.2 %copy-start.9 = (bf16[96,512]{1,0:T(8,128)(2,1)S(1)}, bf16[96,512]{1,0:T(8,128)(2,1)}, u32[]{:S(2)}) copy-start(bf16[96,512]{1,0:T(8,128)(2,1)} %param.10) | copy-start | bytes 294916
  37.9 29.5 %all-to-all-start.1 = ((bf16[96,16,256]{2,0,1:T(8,128)(2,1)}), bf16[96,16,256]{2,0,1:T(8,128)(2,1)S(1)}, u32[]{:S(2)}, u32[]{:S(2)}) async-start(bf16[96,16,256]{2,0,1:T(8,128)(2,1)} %all_gather.13), calls=%async_computation.1 | async-start | bytes 1572864 | tf_op jit(solution)/shard_map/all_to_all | solution.py:93
  67.3 24.4 %all-to-all-start = ((bf16[96,16,256]{2,0,1:T(8,128)(2,1)}), bf16[96,16,256]{2,0,1:T(8,128)(2,1)S(1)}, u32[]{:S(2)}, u32[]{:S(2)}) async-start(bf16[96,16,256]{2,0,1:T(8,128)(2,1)} %all_gather.12), calls=%async_computation | async-start | bytes 1572864 | tf_op jit(solution)/shard_map/all_to_all | solution.py:94
  73.1 102.4 %reduce-scatter.3.cloned.1.call-start = ((), (), s32[]{:S(2)}) async-start(), calls=%async_computation.5 | async-start | bytes 2359296 | tf_op jit(solution)/shard_map/reduce_scatter | solution.py:108
  91.8 5.1 %copy-start.2 = (bf16[96,16,256]{2,0,1:T(8,128)(2,1)}, bf16[96,16,256]{2,0,1:T(8,128)(2,1)S(1)}, u32[]{:S(2)}) copy-start(bf16[96,16,256]{2,0,1:T(8,128)(2,1)S(1)} %all-to-all-done) | copy-start | bytes 2359300
  96.9 0.9 copy-start.13
  148.9 71.2 %all-gather.3.cloned.1.call-start = ((), (), s32[]{:S(2)}) async-start(), calls=%async_computation.6 | async-start | bytes 1671168 | tf_op jit(solution)/shard_map/all_gather | solution.py:119
  178.2 5.7 %copy-start.4 = (f32[512,96]{0,1:T(8,128)}, f32[512,96]{0,1:T(8,128)S(1)}, u32[]{:S(2)}) copy-start(f32[512,96]{0,1:T(8,128)S(1)} %copy.59) | copy-start | bytes 589828
  179.4 8.9 %copy-start.6 = (f32[512,96]{0,1:T(8,128)}, f32[512,96]{0,1:T(8,128)S(1)}, u32[]{:S(2)}) copy-start(f32[512,96]{0,1:T(8,128)S(1)} %copy.60) | copy-start | bytes 589828
  180.2 69.9 %all-gather.5.cloned.1.call-start = ((), (), s32[]{:S(2)}) async-start(), calls=%async_computation.7 | async-start | bytes 2211840 | tf_op jit(solution)/shard_map/all_gather | solution.py:117
  180.4 8.0 %collective-permute-start.2 = (bf16[96,2]{1,0:T(8,128)(2,1)S(1)}, bf16[96,2]{1,0:T(8,128)(2,1)S(1)}, u32[]{:S(2)}, u32[]{:S(2)}) collective-permute-start(bf16[96,2]{1,0:T(8,128)(2,1)S(1)} %get-tuple-element.11), channel_id=1, source_target_pairs={{0,16},{1,17},{2,18},{3,19},{4,20},{5,21},{6,22},{7,23},{8,24},{9,... | collective-permute-start | bytes 1160 | tf_op jit(solution)/shard_map/ppermute | solution.py:15
  182.6 5.7 %collective-permute-start.3 = (bf16[96,2]{1,0:T(8,128)(2,1)S(1)}, bf16[96,2]{1,0:T(8,128)(2,1)S(1)}, u32[]{:S(2)}, u32[]{:S(2)}) collective-permute-start(bf16[96,2]{1,0:T(8,128)(2,1)S(1)} %get-tuple-element.10), channel_id=1, source_target_pairs={{16,0},{17,1},{18,2},{19,3},{20,4},{21,5},{22,6},{23,7},{24,8},{25... | collective-permute-start | bytes 1160 | tf_op jit(solution)/shard_map/ppermute | solution.py:17
  183.9 96.1 %reduce-scatter.5.cloned.1.call-start = ((), (), s32[]{:S(2)}) async-start(), calls=%async_computation.8 | async-start | bytes 2211840 | tf_op jit(solution)/shard_map/reduce_scatter | solution.py:139
  220.1 2.9 copy-start
  228.3 5.0 %copy-start.3 = (bf16[96,16,256]{2,0,1:T(8,128)(2,1)S(1)}, bf16[96,16,256]{2,0,1:T(8,128)(2,1)}, u32[]{:S(2)}) copy-start(bf16[96,16,256]{2,0,1:T(8,128)(2,1)} %copy-done.2) | copy-start | bytes 2359300
  228.3 5.0 %copy-start.14 = (f32[1536,256]{0,1:T(8,128)S(1)}, f32[1536,256]{0,1:T(8,128)}, u32[]{:S(2)}) copy-start(f32[1536,256]{0,1:T(8,128)} %fusion.14) | copy-start | bytes 4718596
  238.2 17.1 %collective-permute-start = (bf16[1536,2]{1,0:T(8,128)(2,1)}, bf16[1536,2]{1,0:T(8,128)(2,1)}, u32[]{:S(2)}, u32[]{:S(2)}) collective-permute-start(bf16[1536,2]{1,0:T(8,128)(2,1)} %get-tuple-element.6), channel_id=1, source_target_pairs={{16,0},{17,1},{18,2},{19,3},{20,4},{21,5},{22,6},{23,7},{24,8},{25... | collective-permute-start | bytes 18440 | tf_op jit(solution)/shard_map/ppermute | solution.py:17
  239.5 14.1 %collective-permute-start.1 = (bf16[1536,2]{1,0:T(8,128)(2,1)}, bf16[1536,2]{1,0:T(8,128)(2,1)}, u32[]{:S(2)}, u32[]{:S(2)}) collective-permute-start(bf16[1536,2]{1,0:T(8,128)(2,1)} %get-tuple-element.7), channel_id=1, source_target_pairs={{0,16},{1,17},{2,18},{3,19},{4,20},{5,21},{6,22},{7,23},{8,24},{9,... | collective-permute-start | bytes 18440 | tf_op jit(solution)/shard_map/ppermute | solution.py:15
  250.1 3.5 %copy-start.11 = (bf16[5,96,1536]{2,1,0:T(8,128)(2,1)S(1)}, bf16[5,96,1536]{2,1,0:T(8,128)(2,1)}, u32[]{:S(2)}) copy-start(bf16[5,96,1536]{2,1,0:T(8,128)(2,1)} %all-gather.5.cloned.1.call-done) | copy-start | bytes 4423684
  257.0 0.9 copy-start.5
  257.0 1.0 copy-start.7
  257.0 1.1 copy-start.10
  (1 other events, 0.7 us)
Sparse Core Ops, SparseCore 0:
  149.0 26.4 reduce-scatter.2
  180.4 39.6 all-gather.2
  221.7 28.3 all-gather.4
  252.9 27.0 reduce-scatter.4
where the time goes:
time: 290 us; the launch traced here: 289 us
  waiting for transfers between devices  102 us (35%)
  blocking collectives  66.6 us (23%)
  matrix products  38.7 us (13%)
  local copies, waits for them, and re-layouts  34.8 us (12%)
  starting transfers between devices  23.1 us (8%)
  between operations  14.3 us (5%)
  other arithmetic  9.54 us (3%)
    all_to_all x1, blocking collectives, local(): lax.all_to_all(rows_back.reshape(model_width, 1, total_rows), 'exp', spli...  41.4 us
    all_gather x1, waiting for transfers between devices, local(): gathered = lax.all_gather(grad_pre_conv, 'exp', axis=0, tiled=True)  31.7 us
    reduce_scatter x1, waiting for transfers between devices, local(): lax.psum_scatter(moved_back, 'ctx', scatter_dimension=2, tiled=True)  26.2 us
    dot_general x8, matrix products, turned(): lax.dot_general(left.astype(jnp.float32), right.astype(jnp.float32), (dim...  21.9 us
    reduce_scatter x1, waiting for transfers between devices, local(): lax.psum_scatter(conv_grad.astype(jnp.bfloat16), 'ctx', scatter_dimension...  19.5 us
    all_to_all x1, waiting for transfers between devices, local(): lax.all_to_all(copied[1], 'exp', split_axis=1, concat_axis=0, tiled=True)  13.8 us
    all_gather x1, blocking collectives, local(): lax.all_gather(send_rows, 'ctx', axis=2, tiled=True)  13 us
    all_gather x1, blocking collectives, local(): lax.all_gather(send_grad, 'ctx', axis=2, tiled=True)  12.2 us
  transfers between devices with their start and end apart: 10, of which 7 were waited for; matrix products, arithmetic and copies ran while one was open for 15% of the time, Pallas kernels for 0%

commit v1 on v0

--- a/solution.py
+++ b/solution.py
@@ -116,7 +116,21 @@
     grad_pre_conv = (grad_total * gelu_slope(pre_float)).astype(jnp.bfloat16)
     full_weight = lax.all_gather(conv_weight, "ctx", axis=2, tiled=True)
     rim_inputs = with_halo(inputs, (("ctx", 1),), margin)
-    gathered = lax.all_gather(grad_pre_conv, "exp", axis=0, tiled=True)
+    ways, here, step = (lax.axis_size("exp"), lax.axis_index("exp"), grad_pre_conv.shape[0])
+    lengths = [n * ways if d == 0 else n for d, n in enumerate(grad_pre_conv.shape)]
+    full = lax.dynamic_update_slice_in_dim(
+        jnp.zeros(lengths, grad_pre_conv.dtype), grad_pre_conv, here * step, axis=0
+    )
+    going_up = going_down = grad_pre_conv
+    for far in range(1, ways // 2 + 1):
+        going_up = lax.ppermute(going_up, "exp", [(d, (d + 1) % ways) for d in range(ways)])
+        full = lax.dynamic_update_slice_in_dim(full, going_up, (here - far) % ways * step, axis=0)
+        if 2 * far < ways:
+            going_down = lax.ppermute(going_down, "exp", [(d, (d - 1) % ways) for d in range(ways)])
+            full = lax.dynamic_update_slice_in_dim(
+                full, going_down, (here + far) % ways * step, axis=0
+            )
+    gathered = full
     rim_grad = with_halo(gathered, (("ctx", 1),), margin)
     conv_back = jnp.zeros((channels, bins_local), jnp.float32)
     tap_grads = []

time: 290 us -> 279 us (0.962)
  waiting for transfers between devices: 102 us -> 69.4 us
  starting transfers between devices: 23.1 us -> 53.7 us
  matrix products: 38.7 us -> 31.3 us
    all_gather x1 -> x0, waiting for transfers between devices: 31.7 us -> none  [local(): gathered = lax.all_gather(grad_pre_conv, 'exp', axis=0, tiled=True)]
    ppermute x0 -> x15, starting transfers between devices: none -> 31.6 us  [the longest x7 31.6 us: local(): lax.ppermute(going_down, 'exp', [(d, (d - 1) % ways) for d in range(ways)])]
    ppermute x0 -> x15, waiting for transfers between devices: none -> 22.3 us  [the longest x8 21.9 us: local(): lax.ppermute(going_up, 'exp', [(d, (d + 1) % ways) for d in range(ways)])]
    reduce_scatter x1, waiting for transfers between devices: 19.5 us -> 0.01 us  [local(): lax.psum_scatter(conv_grad.astype(jnp.bfloat16), 'ctx', scatter_dimension...]
    ppermute x2, waiting for transfers between devices: 2.01 us -> 10.7 us  [with_halo(): lax.ppermute(tail, axis, [(i, (i + 1) % count) for i in range(ends)])]
    reduce_scatter x1, waiting for transfers between devices: 26.2 us -> 19 us  [local(): lax.psum_scatter(moved_back, 'ctx', scatter_dimension=2, tiled=True)]
    dot_general x8, matrix products: 21.9 us -> 15.8 us  [turned(): lax.dot_general(left.astype(jnp.float32), right.astype(jnp.float32), (dim...]
    all_gather x1, waiting for transfers between devices: 4.49 us -> 0.02 us  [local(): full_weight = lax.all_gather(conv_weight, 'ctx', axis=2, tiled=True)]
  transfers between devices with their start and end apart: 10 -> 24, of which waited for: 7 -> 14; matrix products, arithmetic and copies ran while one was open for 15% -> 14% of each run, Pallas kernels for 0% -> 0%
where the time goes in v1:
time: 279 us; the launch traced here: 278 us
  waiting for transfers between devices  69.4 us (25%)
  blocking collectives  66.6 us (24%)
  starting transfers between devices  53.7 us (19%)
  local copies, waits for them, and re-layouts  32.3 us (12%)
  matrix products  31.3 us (11%)
  between operations  14.8 us (5%)
  other arithmetic  9.83 us (4%)
    all_to_all x1, blocking collectives, local(): lax.all_to_all(rows_back.reshape(model_width, 1, total_rows), 'exp', spli...  41.4 us
    ppermute x7, starting transfers between devices, local(): lax.ppermute(going_down, 'exp', [(d, (d - 1) % ways) for d in range(ways)])  31.6 us
    ppermute x8, waiting for transfers between devices, local(): lax.ppermute(going_up, 'exp', [(d, (d + 1) % ways) for d in range(ways)])  21.9 us
    reduce_scatter x1, waiting for transfers between devices, local(): lax.psum_scatter(moved_back, 'ctx', scatter_dimension=2, tiled=True)  19 us
    dot_general x8, matrix products, turned(): lax.dot_general(left.astype(jnp.float32), right.astype(jnp.float32), (dim...  15.8 us
    all_to_all x1, waiting for transfers between devices, local(): lax.all_to_all(copied[1], 'exp', split_axis=1, concat_axis=0, tiled=True)  14.9 us
    all_gather x1, blocking collectives, local(): lax.all_gather(send_rows, 'ctx', axis=2, tiled=True)  13 us
    all_gather x1, blocking collectives, local(): lax.all_gather(send_grad, 'ctx', axis=2, tiled=True)  12.2 us
  transfers between devices with their start and end apart: 24, of which 14 were waited for; matrix products, arithmetic and copies ran while one was open for 14% of the time, Pallas kernels for 0%

profile of v1, /device:TPU:0, one launch (start us, length us, event | category | flops | bytes accessed | tf_op | source)
XLA Modules:
  0.0 277.9 jit_solution(1638088889270176189)
XLA Ops:
  9.5 4.5 %reduce-window.6 = s32[16,8,128]{2,1,0:T(8,128)S(1)} reduce-window(s32[16,8,128]{2,1,0:T(8,128)S(1)} %fusion.81, s32[]{:T(128)} %constant.131.clone.1), window={size=1x1x128 pad=0_0x0_0x127_0}, to_apply=%region_0.0 | reduce-window | flops 2080768 | bytes 131076 | tf_op jit(solution)/shard_map/reduce-window
  14.9 4.3 %scatter_custom_fusion = s32[2048]{0:T(1024)S(1)} fusion(s32[1024]{0:T(1024)S(1)} %bitcast.160, s32[1024]{0:T(1024)S(1)} %add_select_fusion, s32[]{:T(128)} %constant.129.clone.1), kind=kCustom, calls=%fused_computation.147 | custom fusion | bytes 8196 | tf_op jit(solution)/shard_map/scatter | solution.py:73
  19.3 6.2 %gather_fusion.1 = bf16[2048,96]{1,0:T(8,128)(2,1)S(1)} fusion(bf16[96,513]{0,1:T(8,128)(2,1)S(1)} %concatenate.25.clone, s32[2048]{0:T(1024)S(1)} %fusion.82), kind=kCustom, calls=%fused_computation.1 | custom fusion | bytes 794624 | tf_op jit(solution)/shard_map/gather | solution.py:79
  25.8 13.0 %all_gather.10 = bf16[96,16,256]{2,0,1:T(8,128)(2,1)} all-gather(bf16[96,16,128]{2,0,1:T(8,128)(2,1)S(1)} %copy.56), channel_id=1, replica_groups=mesh['ctx'=2,'exp'=16] {'ctx'}, dimensions={2}, use_global_device_ids=true | all-gather | bytes 1179648 | tf_op jit(solution)/shard_map/all_gather | solution.py:89
  38.7 6.2 %all-to-all-start.1 = ((bf16[96,16,256]{2,0,1:T(8,128)(2,1)}), bf16[96,16,256]{2,0,1:T(8,128)(2,1)S(1)}, u32[]{:S(2)}, u32[]{:S(2)}) async-start(bf16[96,16,256]{2,0,1:T(8,128)(2,1)} %all_gather.10), calls=%async_computation.1 | async-start | bytes 1572864 | tf_op jit(solution)/shard_map/all_to_all | solution.py:93
  45.4 4.3 %scatter_custom_fusion.1 = f32[2048]{0:T(1024)S(1)} fusion(s32[1024]{0:T(1024)S(1)} %bitcast.161, f32[1024]{0:T(1024)S(1)} %reshape.134, f32[]{:T(128)} %constant.128.clone.1), kind=kCustom, calls=%fused_computation.129 | custom fusion | bytes 8196 | tf_op jit(solution)/shard_map/scatter | solution.py:75
  49.7 5.5 %gather_fusion = f32[2048,96]{1,0:T(8,128)S(1)} fusion(f32[96,513]{0,1:T(8,128)S(1)} %concatenate.24.clone, s32[2048]{0:T(1024)S(1)} %fusion.82), kind=kCustom, calls=%fused_computation | custom fusion | bytes 1581056 | tf_op jit(solution)/shard_map/gather | solution.py:81
  55.6 12.2 %all_gather.9 = bf16[96,16,256]{2,0,1:T(8,128)(2,1)} all-gather(bf16[96,16,128]{2,0,1:T(8,128)(2,1)S(1)} %multiply_convert_fusion.2), channel_id=1, replica_groups=mesh['ctx'=2,'exp'=16] {'ctx'}, dimensions={2}, use_global_device_ids=true | all-gather | bytes 1179648 | tf_op jit(solution)/shard_map/all_gather | solution.py:90
  67.9 5.7 %all-to-all-start = ((bf16[96,16,256]{2,0,1:T(8,128)(2,1)}), bf16[96,16,256]{2,0,1:T(8,128)(2,1)S(1)}, u32[]{:S(2)}, u32[]{:S(2)}) async-start(bf16[96,16,256]{2,0,1:T(8,128)(2,1)} %all_gather.9), calls=%async_computation | async-start | bytes 1572864 | tf_op jit(solution)/shard_map/all_to_all | solution.py:94
  77.4 14.9 %all-to-all-done = bf16[96,16,256]{2,0,1:T(8,128)(2,1)S(1)} async-done(((bf16[96,16,256]{2,0,1:T(8,128)(2,1)}), bf16[96,16,256]{2,0,1:T(8,128)(2,1)S(1)}, u32[]{:S(2)}, u32[]{:S(2)}) %all-to-all-start) | async-done | bytes 786464 | tf_op jit(solution)/shard_map/all_to_all | solution.py:94
  92.3 4.6 %fusion.20 = bf16[1536,256]{0,1:T(8,128)(2,1)S(1)} fusion(bf16[1536,256]{1,0:T(8,128)(2,1)S(1)} %bitcast.154, bf16[1,1536,1536]{2,1,0:T(8,128)(2,1)} %param.15, f32[1536,256]{0,1:T(8,128)S(1)} %fusion.14), kind=kOutput, calls=%fused_computation.20 | convolution fusion | flops 1215430656 | bytes 7864320 | tf_op jit(solution)/shard_map/dot_general | solution.py:50
  102.8 41.4 %all_to_all.48 = f32[1536,1,256]{2,1,0:T(1,128)S(1)} all-to-all(f32[1536,1,256]{2,1,0:T(1,128)S(1)} %copy.57), channel_id=1, replica_groups=mesh['ctx'=2,'exp'=16] {'exp'}, dimensions={0} | all-to-all | bytes 3145728 | tf_op jit(solution)/shard_map/all_to_all | solution.py:101
  147.6 4.5 %collective-permute-start.17 = (bf16[96,2]{1,0:T(8,128)(2,1)S(1)}, bf16[96,2]{1,0:T(8,128)(2,1)S(1)}, u32[]{:S(2)}, u32[]{:S(2)}) collective-permute-start(bf16[96,2]{1,0:T(8,128)(2,1)S(1)} %get-tuple-element.13), channel_id=1, source_target_pairs={{0,16},{1,17},{2,18},{3,19},{4,20},{5,21},{6,22},{7,23},{8,24},{9,... | collective-permute-start | bytes 1160 | tf_op jit(solution)/shard_map/ppermute | solution.py:15
  153.0 19.0 %reduce-scatter.3.cloned.1.call-done = f32[96,16,128]{2,0,1:T(8,128)} async-done(((f32[96,16,256]{2,0,1:T(8,128)}), f32[96,16,128]{2,0,1:T(8,128)}) %reduce-scatter.3.cloned.1.call-update) | async-done | bytes 786448 | tf_op jit(solution)/shard_map/reduce_scatter | solution.py:108
  176.8 4.4 %collective-permute-start.1 = (bf16[96,512]{1,0:T(8,128)(2,1)S(1)}, bf16[96,512]{1,0:T(8,128)(2,1)S(1)}, u32[]{:S(2)}, u32[]{:S(2)}) collective-permute-start(bf16[96,512]{1,0:T(8,128)(2,1)S(1)} %get-tuple-element.7), channel_id=1, source_target_pairs={{0,15},{1,0},{2,1},{3,2},{4,3},{5,4},{6,5},{7,6},{8,7},{9,8},{10,9... | collective-permute-start | bytes 294920 | tf_op jit(solution)/shard_map/ppermute | solution.py:129
  183.6 4.4 %collective-permute-start.3 = (bf16[96,512]{1,0:T(8,128)(2,1)S(1)}, bf16[96,512]{1,0:T(8,128)(2,1)S(1)}, u32[]{:S(2)}, u32[]{:S(2)}) collective-permute-start(bf16[96,512]{1,0:T(8,128)(2,1)S(1)} %collective-permute-done.1), channel_id=1, source_target_pairs={{0,15},{1,0},{2,1},{3,2},{4,3},{5,4},{6,5},{7,6},{8,7},{9,8},{10,9... | collective-permute-start | bytes 294920 | tf_op jit(solution)/shard_map/ppermute | solution.py:129
  190.4 4.4 %collective-permute-start.5 = (bf16[96,512]{1,0:T(8,128)(2,1)S(1)}, bf16[96,512]{1,0:T(8,128)(2,1)S(1)}, u32[]{:S(2)}, u32[]{:S(2)}) collective-permute-start(bf16[96,512]{1,0:T(8,128)(2,1)S(1)} %collective-permute-done.3), channel_id=1, source_target_pairs={{0,15},{1,0},{2,1},{3,2},{4,3},{5,4},{6,5},{7,6},{8,7},{9,8},{10,9... | collective-permute-start | bytes 294920 | tf_op jit(solution)/shard_map/ppermute | solution.py:129
  197.2 4.4 %collective-permute-start.7 = (bf16[96,512]{1,0:T(8,128)(2,1)S(1)}, bf16[96,512]{1,0:T(8,128)(2,1)S(1)}, u32[]{:S(2)}, u32[]{:S(2)}) collective-permute-start(bf16[96,512]{1,0:T(8,128)(2,1)S(1)} %collective-permute-done.5), channel_id=1, source_target_pairs={{0,15},{1,0},{2,1},{3,2},{4,3},{5,4},{6,5},{7,6},{8,7},{9,8},{10,9... | collective-permute-start | bytes 294920 | tf_op jit(solution)/shard_map/ppermute | solution.py:129
  204.0 4.5 %collective-permute-start.9 = (bf16[96,512]{1,0:T(8,128)(2,1)S(1)}, bf16[96,512]{1,0:T(8,128)(2,1)S(1)}, u32[]{:S(2)}, u32[]{:S(2)}) collective-permute-start(bf16[96,512]{1,0:T(8,128)(2,1)S(1)} %collective-permute-done.7), channel_id=1, source_target_pairs={{0,15},{1,0},{2,1},{3,2},{4,3},{5,4},{6,5},{7,6},{8,7},{9,8},{10,9... | collective-permute-start | bytes 294920 | tf_op jit(solution)/shard_map/ppermute | solution.py:129
  210.7 4.6 %collective-permute-start.11 = (bf16[96,512]{1,0:T(8,128)(2,1)S(1)}, bf16[96,512]{1,0:T(8,128)(2,1)S(1)}, u32[]{:S(2)}, u32[]{:S(2)}) collective-permute-start(bf16[96,512]{1,0:T(8,128)(2,1)S(1)} %collective-permute-done.9), channel_id=1, source_target_pairs={{0,15},{1,0},{2,1},{3,2},{4,3},{5,4},{6,5},{7,6},{8,7},{9,8},{10,9... | collective-permute-start | bytes 294920 | tf_op jit(solution)/shard_map/ppermute | solution.py:129
  217.6 4.6 %collective-permute-start.13 = (bf16[96,512]{1,0:T(8,128)(2,1)S(1)}, bf16[96,512]{1,0:T(8,128)(2,1)S(1)}, u32[]{:S(2)}, u32[]{:S(2)}) collective-permute-start(bf16[96,512]{1,0:T(8,128)(2,1)S(1)} %collective-permute-done.11), channel_id=1, source_target_pairs={{0,15},{1,0},{2,1},{3,2},{4,3},{5,4},{6,5},{7,6},{8,7},{9,8},{10,9... | collective-permute-start | bytes 294920 | tf_op jit(solution)/shard_map/ppermute | solution.py:129
  224.4 6.5 %collective-permute-done.14 = bf16[96,512]{1,0:T(8,128)(2,1)S(1)} collective-permute-done((bf16[96,512]{1,0:T(8,128)(2,1)S(1)}, bf16[96,512]{1,0:T(8,128)(2,1)S(1)}, u32[]{:S(2)}, u32[]{:S(2)}) %collective-permute-start.14) | collective-permute-done | bytes 98336 | tf_op jit(solution)/shard_map/ppermute | solution.py:126
  235.2 5.5 %fusion.1 = bf16[1,1536,1536]{2,1,0:T(8,128)(2,1)} fusion(bf16[1536,256]{1,0:T(8,128)(2,1)} %bitcast.155, f32[1536,256]{0,1:T(8,128)} %copy-done.16), kind=kOutput, calls=%fused_computation.9 | convolution fusion | flops 1213857792 | bytes 7077888 | tf_op jit(solution)/shard_map/dot_general | solution.py:38
  248.7 10.7 %collective-permute-done.16 = bf16[1536,2]{1,0:T(8,128)(2,1)S(1)} collective-permute-done((bf16[1536,2]{1,0:T(8,128)(2,1)S(1)}, bf16[1536,2]{1,0:T(8,128)(2,1)S(1)}, u32[]{:S(2)}, u32[]{:S(2)}) %collective-permute-start.16) | collective-permute-done | bytes 6176 | tf_op jit(solution)/shard_map/ppermute | solution.py:15
  (144 shorter events, 62.5 us)
Async XLA Ops:
  38.7 29.1 %all-to-all-start.1 = ((bf16[96,16,256]{2,0,1:T(8,128)(2,1)}), bf16[96,16,256]{2,0,1:T(8,128)(2,1)S(1)}, u32[]{:S(2)}, u32[]{:S(2)}) async-start(bf16[96,16,256]{2,0,1:T(8,128)(2,1)} %all_gather.10), calls=%async_computation.1 | async-start | bytes 1572864 | tf_op jit(solution)/shard_map/all_to_all | solution.py:93
  67.9 24.4 %all-to-all-start = ((bf16[96,16,256]{2,0,1:T(8,128)(2,1)}), bf16[96,16,256]{2,0,1:T(8,128)(2,1)S(1)}, u32[]{:S(2)}, u32[]{:S(2)}) async-start(bf16[96,16,256]{2,0,1:T(8,128)(2,1)} %all_gather.9), calls=%async_computation | async-start | bytes 1572864 | tf_op jit(solution)/shard_map/all_to_all | solution.py:94
  73.6 98.4 %reduce-scatter.3.cloned.1.call-start = ((), (), s32[]{:S(2)}) async-start(), calls=%async_computation.5 | async-start | bytes 2359296 | tf_op jit(solution)/shard_map/reduce_scatter | solution.py:108
  145.4 103.3 %all-gather.2.cloned.1.call-start = ((), (), s32[]{:S(2)}) async-start(), calls=%async_computation.6 | async-start | bytes 2211840 | tf_op jit(solution)/shard_map/all_gather | solution.py:117
  146.3 34.9 %collective-permute-start.18 = (bf16[96,2]{1,0:T(8,128)(2,1)S(1)}, bf16[96,2]{1,0:T(8,128)(2,1)S(1)}, u32[]{:S(2)}, u32[]{:S(2)}) collective-permute-start(bf16[96,2]{1,0:T(8,128)(2,1)S(1)} %get-tuple-element.12), channel_id=1, source_target_pairs={{16,0},{17,1},{18,2},{19,3},{20,4},{21,5},{22,6},{23,7},{24,8},{25... | collective-permute-start | bytes 1160 | tf_op jit(solution)/shard_map/ppermute | solution.py:17
  147.6 83.3 %collective-permute-start.17 = (bf16[96,2]{1,0:T(8,128)(2,1)S(1)}, bf16[96,2]{1,0:T(8,128)(2,1)S(1)}, u32[]{:S(2)}, u32[]{:S(2)}) collective-permute-start(bf16[96,2]{1,0:T(8,128)(2,1)S(1)} %get-tuple-element.13), channel_id=1, source_target_pairs={{0,16},{1,17},{2,18},{3,19},{4,20},{5,21},{6,22},{7,23},{8,24},{9,... | collective-permute-start | bytes 1160 | tf_op jit(solution)/shard_map/ppermute | solution.py:15
  152.2 116.8 %reduce-scatter.5.cloned.1.call-start = ((), (), s32[]{:S(2)}) async-start(), calls=%async_computation.7 | async-start | bytes 2211840 | tf_op jit(solution)/shard_map/reduce_scatter | solution.py:153
  176.7 6.9 %collective-permute-start = (bf16[96,512]{1,0:T(8,128)(2,1)S(1)}, bf16[96,512]{1,0:T(8,128)(2,1)S(1)}, u32[]{:S(2)}, u32[]{:S(2)}) collective-permute-start(bf16[96,512]{1,0:T(8,128)(2,1)S(1)} %get-tuple-element.7), channel_id=1, source_target_pairs={{0,1},{1,2},{2,3},{3,4},{4,5},{5,6},{6,7},{7,8},{8,9},{9,10},{10,1... | collective-permute-start | bytes 294920 | tf_op jit(solution)/shard_map/ppermute | solution.py:126
  176.8 6.8 %collective-permute-start.1 = (bf16[96,512]{1,0:T(8,128)(2,1)S(1)}, bf16[96,512]{1,0:T(8,128)(2,1)S(1)}, u32[]{:S(2)}, u32[]{:S(2)}) collective-permute-start(bf16[96,512]{1,0:T(8,128)(2,1)S(1)} %get-tuple-element.7), channel_id=1, source_target_pairs={{0,15},{1,0},{2,1},{3,2},{4,3},{5,4},{6,5},{7,6},{8,7},{9,8},{10,9... | collective-permute-start | bytes 294920 | tf_op jit(solution)/shard_map/ppermute | solution.py:129
  183.6 6.7 %collective-permute-start.2 = (bf16[96,512]{1,0:T(8,128)(2,1)S(1)}, bf16[96,512]{1,0:T(8,128)(2,1)S(1)}, u32[]{:S(2)}, u32[]{:S(2)}) collective-permute-start(bf16[96,512]{1,0:T(8,128)(2,1)S(1)} %collective-permute-done), channel_id=1, source_target_pairs={{0,1},{1,2},{2,3},{3,4},{4,5},{5,6},{6,7},{7,8},{8,9},{9,10},{10,1... | collective-permute-start | bytes 294920 | tf_op jit(solution)/shard_map/ppermute | solution.py:126
  183.6 6.7 %collective-permute-start.3 = (bf16[96,512]{1,0:T(8,128)(2,1)S(1)}, bf16[96,512]{1,0:T(8,128)(2,1)S(1)}, u32[]{:S(2)}, u32[]{:S(2)}) collective-permute-start(bf16[96,512]{1,0:T(8,128)(2,1)S(1)} %collective-permute-done.1), channel_id=1, source_target_pairs={{0,15},{1,0},{2,1},{3,2},{4,3},{5,4},{6,5},{7,6},{8,7},{9,8},{10,9... | collective-permute-start | bytes 294920 | tf_op jit(solution)/shard_map/ppermute | solution.py:129
  190.4 6.8 %collective-permute-start.4 = (bf16[96,512]{1,0:T(8,128)(2,1)S(1)}, bf16[96,512]{1,0:T(8,128)(2,1)S(1)}, u32[]{:S(2)}, u32[]{:S(2)}) collective-permute-start(bf16[96,512]{1,0:T(8,128)(2,1)S(1)} %collective-permute-done.2), channel_id=1, source_target_pairs={{0,1},{1,2},{2,3},{3,4},{4,5},{5,6},{6,7},{7,8},{8,9},{9,10},{10,1... | collective-permute-start | bytes 294920 | tf_op jit(solution)/shard_map/ppermute | solution.py:126
  190.4 6.8 %collective-permute-start.5 = (bf16[96,512]{1,0:T(8,128)(2,1)S(1)}, bf16[96,512]{1,0:T(8,128)(2,1)S(1)}, u32[]{:S(2)}, u32[]{:S(2)}) collective-permute-start(bf16[96,512]{1,0:T(8,128)(2,1)S(1)} %collective-permute-done.3), channel_id=1, source_target_pairs={{0,15},{1,0},{2,1},{3,2},{4,3},{5,4},{6,5},{7,6},{8,7},{9,8},{10,9... | collective-permute-start | bytes 294920 | tf_op jit(solution)/shard_map/ppermute | solution.py:129
  197.2 6.7 %collective-permute-start.6 = (bf16[96,512]{1,0:T(8,128)(2,1)S(1)}, bf16[96,512]{1,0:T(8,128)(2,1)S(1)}, u32[]{:S(2)}, u32[]{:S(2)}) collective-permute-start(bf16[96,512]{1,0:T(8,128)(2,1)S(1)} %collective-permute-done.4), channel_id=1, source_target_pairs={{0,1},{1,2},{2,3},{3,4},{4,5},{5,6},{6,7},{7,8},{8,9},{9,10},{10,1... | collective-permute-start | bytes 294920 | tf_op jit(solution)/shard_map/ppermute | solution.py:126
  197.2 6.7 %collective-permute-start.7 = (bf16[96,512]{1,0:T(8,128)(2,1)S(1)}, bf16[96,512]{1,0:T(8,128)(2,1)S(1)}, u32[]{:S(2)}, u32[]{:S(2)}) collective-permute-start(bf16[96,512]{1,0:T(8,128)(2,1)S(1)} %collective-permute-done.5), channel_id=1, source_target_pairs={{0,15},{1,0},{2,1},{3,2},{4,3},{5,4},{6,5},{7,6},{8,7},{9,8},{10,9... | collective-permute-start | bytes 294920 | tf_op jit(solution)/shard_map/ppermute | solution.py:129
  204.0 6.7 %collective-permute-start.8 = (bf16[96,512]{1,0:T(8,128)(2,1)S(1)}, bf16[96,512]{1,0:T(8,128)(2,1)S(1)}, u32[]{:S(2)}, u32[]{:S(2)}) collective-permute-start(bf16[96,512]{1,0:T(8,128)(2,1)S(1)} %collective-permute-done.6), channel_id=1, source_target_pairs={{0,1},{1,2},{2,3},{3,4},{4,5},{5,6},{6,7},{7,8},{8,9},{9,10},{10,1... | collective-permute-start | bytes 294920 | tf_op jit(solution)/shard_map/ppermute | solution.py:126
  204.0 6.8 %collective-permute-start.9 = (bf16[96,512]{1,0:T(8,128)(2,1)S(1)}, bf16[96,512]{1,0:T(8,128)(2,1)S(1)}, u32[]{:S(2)}, u32[]{:S(2)}) collective-permute-start(bf16[96,512]{1,0:T(8,128)(2,1)S(1)} %collective-permute-done.7), channel_id=1, source_target_pairs={{0,15},{1,0},{2,1},{3,2},{4,3},{5,4},{6,5},{7,6},{8,7},{9,8},{10,9... | collective-permute-start | bytes 294920 | tf_op jit(solution)/shard_map/ppermute | solution.py:129
  210.7 6.8 %collective-permute-start.10 = (bf16[96,512]{1,0:T(8,128)(2,1)S(1)}, bf16[96,512]{1,0:T(8,128)(2,1)S(1)}, u32[]{:S(2)}, u32[]{:S(2)}) collective-permute-start(bf16[96,512]{1,0:T(8,128)(2,1)S(1)} %collective-permute-done.8), channel_id=1, source_target_pairs={{0,1},{1,2},{2,3},{3,4},{4,5},{5,6},{6,7},{7,8},{8,9},{9,10},{10,1... | collective-permute-start | bytes 294920 | tf_op jit(solution)/shard_map/ppermute | solution.py:126
  210.7 6.8 %collective-permute-start.11 = (bf16[96,512]{1,0:T(8,128)(2,1)S(1)}, bf16[96,512]{1,0:T(8,128)(2,1)S(1)}, u32[]{:S(2)}, u32[]{:S(2)}) collective-permute-start(bf16[96,512]{1,0:T(8,128)(2,1)S(1)} %collective-permute-done.9), channel_id=1, source_target_pairs={{0,15},{1,0},{2,1},{3,2},{4,3},{5,4},{6,5},{7,6},{8,7},{9,8},{10,9... | collective-permute-start | bytes 294920 | tf_op jit(solution)/shard_map/ppermute | solution.py:129
  217.5 6.7 %collective-permute-start.12 = (bf16[96,512]{1,0:T(8,128)(2,1)S(1)}, bf16[96,512]{1,0:T(8,128)(2,1)S(1)}, u32[]{:S(2)}, u32[]{:S(2)}) collective-permute-start(bf16[96,512]{1,0:T(8,128)(2,1)S(1)} %collective-permute-done.10), channel_id=1, source_target_pairs={{0,1},{1,2},{2,3},{3,4},{4,5},{5,6},{6,7},{7,8},{8,9},{9,10},{10,1... | collective-permute-start | bytes 294920 | tf_op jit(solution)/shard_map/ppermute | solution.py:126
  217.6 6.8 %collective-permute-start.13 = (bf16[96,512]{1,0:T(8,128)(2,1)S(1)}, bf16[96,512]{1,0:T(8,128)(2,1)S(1)}, u32[]{:S(2)}, u32[]{:S(2)}) collective-permute-start(bf16[96,512]{1,0:T(8,128)(2,1)S(1)} %collective-permute-done.11), channel_id=1, source_target_pairs={{0,15},{1,0},{2,1},{3,2},{4,3},{5,4},{6,5},{7,6},{8,7},{9,8},{10,9... | collective-permute-start | bytes 294920 | tf_op jit(solution)/shard_map/ppermute | solution.py:129
  224.2 6.7 %collective-permute-start.14 = (bf16[96,512]{1,0:T(8,128)(2,1)S(1)}, bf16[96,512]{1,0:T(8,128)(2,1)S(1)}, u32[]{:S(2)}, u32[]{:S(2)}) collective-permute-start(bf16[96,512]{1,0:T(8,128)(2,1)S(1)} %collective-permute-done.12), channel_id=1, source_target_pairs={{0,1},{1,2},{2,3},{3,4},{4,5},{5,6},{6,7},{7,8},{8,9},{9,10},{10,1... | collective-permute-start | bytes 294920 | tf_op jit(solution)/shard_map/ppermute | solution.py:126
  240.9 18.5 %collective-permute-start.16 = (bf16[1536,2]{1,0:T(8,128)(2,1)S(1)}, bf16[1536,2]{1,0:T(8,128)(2,1)S(1)}, u32[]{:S(2)}, u32[]{:S(2)}) collective-permute-start(bf16[1536,2]{1,0:T(8,128)(2,1)S(1)} %get-tuple-element.9), channel_id=1, source_target_pairs={{0,16},{1,17},{2,18},{3,19},{4,20},{5,21},{6,22},{7,23},{8,24},{9,... | collective-permute-start | bytes 18440 | tf_op jit(solution)/shard_map/ppermute | solution.py:15
  247.4 16.9 %collective-permute-start.15 = (bf16[1536,2]{1,0:T(8,128)(2,1)S(1)}, bf16[1536,2]{1,0:T(8,128)(2,1)}, u32[]{:S(2)}, u32[]{:S(2)}) collective-permute-start(bf16[1536,2]{1,0:T(8,128)(2,1)S(1)} %get-tuple-element.8), channel_id=1, source_target_pairs={{16,0},{17,1},{18,2},{19,3},{20,4},{21,5},{22,6},{23,7},{24,8},{25... | collective-permute-start | bytes 18440 | tf_op jit(solution)/shard_map/ppermute | solution.py:17
  (17 other events, 162.9 us)
Sparse Core Ops, SparseCore 0:
  145.5 26.4 reduce-scatter.2
  173.6 26.3 all-gather.1
  235.4 28.5 reduce-scatter.4
